TPU v7x, 512 devices: a whole 4x4x16 slice. The times are simulated.
512 devices in a mesh: group: 32 (over z, core), member: 16 (over y, x).
Axes of the slice: x: 4, y: 4, z: 16, core: 2. Of those that a mesh axis runs over, the one named last changes fastest.
Arguments:
- route_group: int32 [2048, 4], P('group'), may hold values from 0 to 31, all different within a row; in each aligned block of 64 rows (0 to 63, 64 to 127, ...) at most 10 rows name the same one
- expert_pick: int32 [2048, 4, 2], P('group'), may hold values 0 or 1
- route_score: float32 [2048, 4, 2], P('group'), may hold values from 0.1 to 1
- expert_hidden: bfloat16 [32, 320, 4096], P('group', 'member'), may hold values from -6 to 6
- down_weight: bfloat16 [32, 2, 2048, 7168], P('group', None, None, 'member'), may hold values from -0.125 to 0.125
Outputs:
- combined: bfloat16 [2048, 7168], P('group', 'member')
Inputs may be any that keep to these rules, and one draw needn't show every extreme that they name: `route_group`: within the 64 tokens of one home group (aligned blocks of rows) a token's 4 groups differ, no group is chosen by more than 10 tokens, a bound that some block reaches.
All inputs are finite; a program needn't handle non-finite values. No bound on the sum of `expert_pick` on one device may be relied on, other than what follows from the above.
Results may differ from a plain program's by a relative error of at most 0.001.
Values may be sent and summed in bfloat16 or wider, within the bound.
A program may use at most 64 MiB of HBM per device.

v0:
```python
import jax
import jax.numpy as jnp
from jax import lax
from jax.sharding import PartitionSpec as P


def per_device(route_group, expert_pick, route_score, expert_hidden, down_weight):
    groups = lax.axis_size("group")
    slot_rows = expert_hidden.shape[1] * lax.axis_size("member")
    caps_rows = slot_rows // groups
    width_part = down_weight.shape[3]
    labels = jnp.arange(groups, dtype=jnp.int32)
    onehot = (route_group[..., None] == labels).astype(jnp.int32)
    per_token = jnp.sum(onehot, axis=1)
    earlier = jnp.cumsum(per_token, axis=0) - per_token
    slot_rank = jnp.take_along_axis(earlier, route_group, axis=1)
    flat_slot = route_group * caps_rows + slot_rank
    coef = route_score * expert_pick.astype(jnp.float32)
    weights = down_weight[0]
    experts = weights.shape[0]
    hidden_units = weights.shape[1]
    piece = lax.all_gather(expert_hidden, "member", axis=1, tiled=True)
    products = []
    for expert in range(experts):
        products.append(
            jnp.dot(
                piece[0, :, expert * hidden_units : (expert + 1) * hidden_units],
                weights[expert],
                preferred_element_type=jnp.float32,
            )
        )
    slot_out = jnp.stack(products, axis=1)
    returned = lax.all_to_all(
        slot_out.reshape(groups, caps_rows, experts, width_part),
        "group",
        split_axis=0,
        concat_axis=0,
        tiled=True,
    )
    picked = returned.reshape(slot_rows, experts, width_part)[flat_slot]
    combined = jnp.sum(jnp.sum(picked * coef[..., None], axis=2), axis=1)
    return combined.astype(jnp.bfloat16)


def solution(mesh):
    placed = (
        P("group", None),
        P("group", None, None),
        P("group", None, None),
        P("group", "member", None),
        P("group", None, None, "member"),
    )
    return jax.shard_map(
        per_device, mesh=mesh, in_specs=placed, out_specs=P("group", "member"), check_vma=False
    )
```

profile of v0, /device:TPU:1, one launch (start us, length us, event | category | flops | bytes accessed | tf_op | source)
XLA Modules:
  0.0 201.4 jit_solution(17581958680643972099)
XLA Ops:
  6.5 2.0 copy.61
  8.5 78.9 %all-gather.2.cloned.1.call-done = bf16[1,320,4096]{2,0,1:T(2,128)(2,1)} async-done(((bf16[1,20,4096]{2,0,1:T(2,128)(2,1)}), bf16[1,320,4096]{2,0,1:T(2,128)(2,1)}) %all-gather.2.cloned.1.call-update) | async-done | bytes 2621456 | tf_op jit(solution)/shard_map/all_gather | solution.py:22
  87.4 12.3 %slice_reduce_fusion.1 = (bf16[320,2048]{1,0:T(8,128)(2,1)S(1)}, bf16[320,2048]{1,0:T(8,128)(2,1)S(1)}) fusion(bf16[1,320,4096]{2,0,1:T(2,128)(2,1)} %all-gather.2.cloned.1.call-done), kind=kLoop, calls=%fused_computation.3 | loop fusion | bytes 5242880 | tf_op jit(solution)/shard_map/slice | solution.py:27
  99.8 1.6 dot_general.17
  101.3 1.5 dot_general.14
  102.9 0.8 copy-done
  103.7 2.7 %fusion.13 = f32[32,10,1,448]{3,0,1,2:T(8,128)S(1)} fusion(bf16[1,2,2048,448]{2,3,1,0:T(8,128)(2,1)} %param.9, bf16[32,10,2048]{2,1,0:T(8,128)(2,1)S(1)} %copy-done), kind=kOutput, calls=%fused_computation.14 | convolution fusion | flops 587202560 | bytes 3719168 | tf_op jit(solution)/shard_map/dot_general | solution.py:26
  106.5 2.6 %fusion.8 = f32[32,10,1,448]{3,0,1,2:T(8,128)S(1)} fusion(bf16[1,2,2048,448]{2,3,1,0:T(8,128)(2,1)} %param.9, bf16[32,10,2048]{2,1,0:T(8,128)(2,1)S(1)} %copy-done.1), kind=kOutput, calls=%fused_computation.13 | convolution fusion | flops 587202560 | bytes 3719168 | tf_op jit(solution)/shard_map/dot_general | solution.py:26
  109.1 0.1 pad_maximum_fusion
  109.2 2.1 %copy.64 = f32[32,10,2,448]{3,2,1,0:T(2,128)} copy(f32[32,10,2,448]{3,0,1,2:T(8,128)S(1)} %pad_maximum_fusion) | data formatting | bytes 2293760 | tf_op jit(solution)/shard_map/stack | solution.py:32
  111.3 13.1 %all-to-all-start = ((f32[32,10,2,448]{3,2,1,0:T(2,128)}), f32[32,10,2,448]{3,2,1,0:T(2,128)S(1)}, u32[]{:S(2)}, u32[]{:S(2)}) async-start(f32[32,10,2,448]{3,2,1,0:T(2,128)} %copy.64), calls=%async_computation | async-start | bytes 2621440 | tf_op jit(solution)/shard_map/all_to_all | solution.py:33
  124.5 0.1 copy.65
  124.5 0.1 reduce_window_sum.11
  124.7 0.1 copy.67
  124.8 0.1 reshape.45
  124.9 1.9 gather_fusion.1
  126.8 0.1 reshape.48
  127.0 0.1 copy.68
  127.0 0.1 copy.69
  127.1 0.1 reshape.39
  127.3 0.1 copy.70
  127.4 63.9 %all-to-all-done = f32[32,10,2,448]{3,2,1,0:T(2,128)S(1)} async-done(((f32[32,10,2,448]{3,2,1,0:T(2,128)}), f32[32,10,2,448]{3,2,1,0:T(2,128)S(1)}, u32[]{:S(2)}, u32[]{:S(2)}) %all-to-all-start) | async-done | bytes 1146912 | tf_op jit(solution)/shard_map/all_to_all | solution.py:33
  191.3 1.8 gather_fusion
  193.1 1.5 multiply_reduce_fusion
  (17 shorter events, 0.1 us)
Async XLA Ops:
  6.5 80.9 %all-gather.2.cloned.1.call-start = ((), (), s32[]{:S(2)}) async-start(), calls=%async_computation.1 | async-start | bytes 5570560 | tf_op jit(solution)/shard_map/all_gather | solution.py:22
  101.3 2.3 %copy-start = (bf16[32,10,2048]{2,1,0:T(8,128)(2,1)S(1)}, bf16[32,10,2048]{2,1,0:T(8,128)(2,1)}, u32[]{:S(2)}) copy-start(bf16[32,10,2048]{2,1,0:T(8,128)(2,1)} %dot_general.17) | copy-start | bytes 3932164
  103.7 2.8 %copy-start.1 = (bf16[32,10,2048]{2,1,0:T(8,128)(2,1)S(1)}, bf16[32,10,2048]{2,1,0:T(8,128)(2,1)}, u32[]{:S(2)}) copy-start(bf16[32,10,2048]{2,1,0:T(8,128)(2,1)} %dot_general.14) | copy-start | bytes 3932164
  111.3 13.2 %copy-start.2 = (s32[64,4]{0,1:T(4,128)S(1)}, s32[64,4]{0,1:T(4,128)}, u32[]{:S(2)}) copy-start(s32[64,4]{0,1:T(4,128)} %param.5) | copy-start | bytes 3076
  111.3 80.0 %all-to-all-start = ((f32[32,10,2,448]{3,2,1,0:T(2,128)}), f32[32,10,2,448]{3,2,1,0:T(2,128)S(1)}, u32[]{:S(2)}, u32[]{:S(2)}) async-start(f32[32,10,2,448]{3,2,1,0:T(2,128)} %copy.64), calls=%async_computation | async-start | bytes 2621440 | tf_op jit(solution)/shard_map/all_to_all | solution.py:33
  124.9 2.4 %copy-start.3 = (f32[64,4,2]{0,2,1:T(2,128)S(1)}, f32[64,4,2]{0,2,1:T(2,128)}, u32[]{:S(2)}) copy-start(f32[64,4,2]{0,2,1:T(2,128)} %param.7) | copy-start | bytes 6148
  124.9 2.4 %copy-start.4 = (s32[64,4,2]{0,2,1:T(2,128)S(1)}, s32[64,4,2]{0,2,1:T(2,128)}, u32[]{:S(2)}) copy-start(s32[64,4,2]{0,2,1:T(2,128)} %param.6) | copy-start | bytes 6148
Sparse Core Ops, SparseCore 0:
  10.4 76.9 all-gather.1
where the time goes:
time: 202 us; the launch traced here: 201 us
  waiting for transfers between devices  143 us (71%)
  local copies, waits for them, and re-layouts  24.8 us (12%)
  between operations  13.5 us (7%)
  starting transfers between devices  13.1 us (6%)
  matrix products  5.34 us (3%)
    all_gather x1, waiting for transfers between devices, per_device(): piece = lax.all_gather(expert_hidden, 'member', axis=1, tiled=True)  78.9 us
    all_to_all x1, waiting for transfers between devices, per_device(): lax.all_to_all(slot_out.reshape(groups, caps_rows, experts, width_part),...  63.9 us
    all_to_all x1, starting transfers between devices, per_device(): lax.all_to_all(slot_out.reshape(groups, caps_rows, experts, width_part),...  13.1 us
    slice x1, local copies, waits for them, and re-layouts, per_device(): piece[0, :, expert * hidden_units:(expert + 1) * hidden_units]  12.3 us
    dot_general x2, matrix products, per_device(): jnp.dot(piece[0, :, expert * hidden_units:(expert + 1) * hidden_units], w...  5.34 us
  transfers between devices with their start and end apart: 2, of which 2 were waited for; matrix products, arithmetic and copies ran while one was open for 1% of the time, Pallas kernels for 0%

commit v1 on v0

v1 whole, which is shorter than its diff:
```python
import functools

import jax
import jax.numpy as jnp
from jax import lax
from jax.experimental import pallas as pl
from jax.experimental.pallas import tpu as pltpu
from jax.sharding import PartitionSpec as P

MESH = pl.DeviceIdType.MESH
NG = 32
NM = 16
ROWS = 8
WIDE = 5120
HALF = WIDE // 2
LANES = 128
MAIN = 64

BATCHES = (
    ((0, 0), (1, 0), (3, 0)),
    ((2, 0), (0, 1), (0, 3)),
    ((1, 1), (3, 1), (1, 3), (3, 3)),
    ((2, 1), (2, 3), (0, 2)),
    ((1, 2), (3, 2), (2, 2)),
)
ORDER = tuple((half, block) for batch in BATCHES for half in (0, 1) for block in batch)


def slot_in_batch(half, first, second):
    slot = jnp.int32(0)
    for batch in BATCHES:
        for index, (du, dv) in enumerate(batch):
            here = (first == du) & (second == dv)
            slot = jnp.where(here, index + half * len(batch), slot)
    return slot


def kernel(
    route_hbm, pick_hbm, score_hbm, hidden_hbm, weight_hbm, out_ref,
    route, pick, score, hidden, weight, blocks, table, table_in, words, words_in, chooser,
    load_sem, gather_send, gather_recv, table_send, table_recv, word_send, word_recv, own_sem,
):
    g = lax.axis_index("group")
    m = lax.axis_index("member")
    z, core = g // 2, g % 2
    y, x = m // 4, m % 4

    loads = [
        pltpu.make_async_copy(source, target, load_sem.at[i])
        for i, (source, target) in enumerate(
            (
                (hidden_hbm, hidden),
                (route_hbm, route),
                (pick_hbm, pick),
                (score_hbm, score),
                (weight_hbm.at[:, pl.ds(0, 224), :], weight.at[:, pl.ds(0, 224), :]),
                (weight_hbm.at[:, pl.ds(224, 224), :], weight.at[:, pl.ds(256, 224), :]),
            )
        )
    ]
    for load in loads:
        load.start()

    def member_at(dx, dy):
        return ((y + dy) % 4) * 4 + (x + dx) % 4

    barrier = pltpu.get_barrier_semaphore()
    for dx, dy in ((1, 0), (3, 0), (0, 1), (0, 3)):
        pl.semaphore_signal(barrier, inc=1, device_id=(g, member_at(dx, dy)), device_id_type=MESH)

    def greet(i, carry):
        pl.semaphore_signal(barrier, inc=1, device_id=((g + i) % NG, m), device_id_type=MESH)
        return carry

    lax.fori_loop(1, NG, greet, 0)

    loads[0].wait()
    for half in (0, 1):
        at = 10 * half
        mine = half * NM + m
        blocks[mine, :, 0:4096] = hidden[at : at + 8, :]
        blocks[mine, :, 4096:WIDE] = jnp.concatenate(
            [hidden[at + 8 : at + 10, q * 1024 : (q + 1) * 1024] for q in range(4)], axis=0
        )

    pl.semaphore_wait(barrier, 4 + NG - 1)

    def offsets(half, du, dv):
        return (du, dv) if half == 0 else (dv, du)

    def slot_of(half, du, dv):
        dx, dy = offsets(half, du, dv)
        return half * NM + member_at(dx, dy)

    def part_of(slot, part):
        if part is None:
            return blocks.at[slot]
        return blocks.at[slot, :, pl.ds(part * HALF, HALF)]

    def copy(half, du, dv, part, su, sv):
        slot = slot_of(half, du, dv)
        ref = part_of(slot, part)
        index = ((half * 4 + (du - su) % 4) * 4 + (dv - sv) % 4) * 2 + (part or 0)
        return pltpu.make_async_remote_copy(
            src_ref=ref,
            dst_ref=ref,
            send_sem=gather_send,
            recv_sem=gather_recv.at[index],
            device_id=(g, member_at(*offsets(half, su, sv))),
            device_id_type=MESH,
        )

    def send(half, du, dv, part, su, sv):
        copy(half, du, dv, part, su, sv).start()

    def arrived(half, du, dv):
        parts = (0, 1) if 2 in (du, dv) and (dv == 2 or dv == 0) else (None,)
        for part in parts:
            slot = slot_of(half, du, dv)
            ref = part_of(slot, part)
            index = ((half * 4 + du) * 4 + dv) * 2 + (part or 0)
            pltpu.make_async_remote_copy(
                src_ref=ref, dst_ref=ref, send_sem=gather_send, recv_sem=gather_recv.at[index],
                device_id=(g, m), device_id_type=MESH,
            ).wait_recv()

    for half in (0, 1):
        send(half, 0, 0, None, 1, 0)
        send(half, 0, 0, None, 3, 0)
    for half in (0, 1):
        send(half, 0, 0, None, 0, 1)
        send(half, 0, 0, None, 0, 3)

    for load in loads[1:4]:
        load.wait()
    group_row = lax.broadcasted_iota(jnp.int32, (NG, 64), 0)
    chosen = [route[k : k + 1, :] == group_row for k in range(4)]
    per_token = sum(c.astype(jnp.float32) for c in chosen)
    before = (
        lax.broadcasted_iota(jnp.int32, (64, 64), 0) < lax.broadcasted_iota(jnp.int32, (64, 64), 1)
    ).astype(jnp.bfloat16)
    earlier = jnp.dot(per_token.astype(jnp.bfloat16), before, preferred_element_type=jnp.float32)
    ranks = [jnp.sum(jnp.where(c, earlier, 0.0), axis=0, keepdims=True) for c in chosen]
    routes = [route[k : k + 1, :].astype(jnp.float32) for k in range(4)]
    turned = jnp.transpose(jnp.concatenate(ranks + routes, axis=0), (1, 0))

    lane = lax.broadcasted_iota(jnp.int32, (1, LANES), 1)
    dx, dy = (z % 4 - x + 4) % 4, (z // 4 - y + 4) % 4
    slot = slot_in_batch(core, jnp.where(core == 0, dx, dy), jnp.where(core == 0, dy, dx))
    inner = lane % 8
    rank_of_lane = jnp.where(
        lane // 8 == slot, inner, jnp.where(lane // 8 == slot + 8, 8 + inner % 2, -1)
    ).astype(jnp.float32)
    total = jnp.zeros((NG, 2 * LANES), jnp.float32)
    for k in range(4):
        hit = (turned[:, k : k + 1] == rank_of_lane).astype(jnp.float32)
        both = []
        for e in range(2):
            coef = score[k, e : e + 1, :] * pick[k, e : e + 1, :].astype(jnp.float32)
            both.append(
                jnp.dot(
                    jnp.where(chosen[k], coef, 0.0), hit,
                    preferred_element_type=jnp.float32, precision=lax.Precision.HIGHEST,
                )
            )
        total = total + jnp.concatenate(both, axis=1)
    table[...] = total.reshape(NG, 1, 2 * LANES)

    def send_table(i, carry):
        to = (g + i) % NG
        pltpu.make_async_remote_copy(
            src_ref=table.at[to], dst_ref=table_in.at[g], send_sem=table_send, recv_sem=table_recv,
            device_id=(to, m), device_id_type=MESH,
        ).start()
        return carry

    lax.fori_loop(1, NG, send_table, 0)
    table_in[g] = table[g]

    row = lax.broadcasted_iota(jnp.int32, (1, 20 * NG), 1)
    piece, inside = (row % 20) // 4, row % 4
    segment = jnp.where(piece == 4, inside // 2, piece // 2)
    rank = jnp.where(piece == 4, 8 + inside % 2, (piece % 2) * 4 + inside)
    key = (10 * (row // 20) + rank).astype(jnp.float32)
    picks = jnp.zeros((64, 20 * NG), jnp.float32)
    for k in range(4):
        token_key = 10.0 * turned[:, 4 + k : 5 + k] + turned[:, k : k + 1]
        picks = picks + (token_key == key).astype(jnp.float32)
    for s in (0, 1):
        chooser[64 * s : 64 * (s + 1), :] = jnp.where(segment == s, picks, 0.0).astype(jnp.bfloat16)

    loads[4].wait()
    loads[5].wait()
    weight[:, 224:256, :] = jnp.zeros((2, 32, 2048), jnp.bfloat16)
    weight[:, 480:512, :] = jnp.zeros((2, 32, 2048), jnp.bfloat16)

    def multiply(batch, first_word):
        todo = [(half, du, dv) for half in (0, 1) for du, dv in batch]
        count = len(todo)
        slots = [slot_of(*block) for block in todo]
        padded = slots + [slots[0]] * (8 - count)
        coefs = None
        for half, du, dv in todo:
            home = 2 * member_at(*offsets(half, du, dv)) + half
            coefs = table_in[home] if coefs is None else coefs + table_in[home]
        each = []
        for q in range(4):
            part = coefs[:, (q // 2) * LANES : (q // 2 + 1) * LANES]
            each.append(jnp.where((lane < MAIN) | (inner // 2 == q), part, 0.0))
        columns = jnp.transpose(jnp.concatenate(each + each, axis=0), (1, 0))
        rest = [blocks[s, :, 4096:WIDE] for s in padded]
        result = None
        for q in range(4):
            left = jnp.concatenate(
                [blocks[s, :, q * 1024 : (q + 1) * 1024] for s in padded] + rest, axis=0
            )
            product = lax.dot_general(
                left, weight[q // 2, :, (q % 2) * 1024 : (q % 2 + 1) * 1024],
                (((1,), (1,)), ((), ())), preferred_element_type=jnp.float32,
            )
            product = product * columns[:, q : q + 1]
            result = product if result is None else result + product
        main = result[0 : 8 * count]
        tail = result[MAIN : MAIN + 8 * count]
        tail = tail + pltpu.roll(tail, 8 * count - 4, 0)
        tail = tail + pltpu.roll(tail, 8 * count - 2, 0)
        for rows, is_tail in ((main, False), (tail, True)):
            for s in (0, 1):
                values = rows[:, 256 * s : 256 * (s + 1)]
                peak = jnp.max(jnp.abs(values), axis=1, keepdims=True)
                power = jnp.ceil(jnp.log2(jnp.maximum(peak, 1e-30) * (1.0 / 32767.0)))
                fixed = values * jnp.exp2(-power)
                fixed = jnp.clip(jnp.round(fixed), -32767.0, 32767.0).astype(jnp.int32)
                high = jnp.where(lane < 96, fixed[:, LANES:], power.astype(jnp.int32))
                packed = (high << 16) | (fixed[:, :LANES] & 0xFFFF)
                for j in range(count):
                    if is_tail:
                        words[first_word + j, 4, 2 * s : 2 * s + 2, :] = packed[8 * j : 8 * j + 2]
                    else:
                        words[first_word + j, 2 * s] = packed[8 * j : 8 * j + 4]
                        words[first_word + j, 2 * s + 1] = packed[8 * j + 4 : 8 * j + 8]
        for j, (half, du, dv) in enumerate(todo):
            home = 2 * member_at(*offsets(half, du, dv)) + half

            @pl.when(home != g)
            def _():
                pltpu.make_async_remote_copy(
                    src_ref=words.at[first_word + j], dst_ref=words_in.at[g],
                    send_sem=word_send, recv_sem=word_recv,
                    device_id=(home, m), device_id_type=MESH,
                ).start()

            @pl.when(home == g)
            def _():
                pltpu.make_async_copy(words.at[first_word + j], words_in.at[g], own_sem).start()

        return first_word + count

    def both(step):
        for half in (0, 1):
            step(half)

    def near_first(half):
        arrived(half, 1, 0)
        arrived(half, 3, 0)
        send(half, 3, 0, 0, 1, 0)
        send(half, 1, 0, 1, 3, 0)
        for du in (1, 3):
            for sv in (1, 3):
                send(half, du, 0, None, 0, sv)

    def across(half, du):
        arrived(half, du, 1)
        arrived(half, du, 3)
        send(half, du, 3, 0, 0, 1)
        send(half, du, 1, 1, 0, 3)

    def far_first(half):
        arrived(half, 2, 0)
        for sv in (1, 3):
            send(half, 2, 0, None, 0, sv)

    def opposite(half, dus):
        for du in dus:
            arrived(half, du, 2)

    both(near_first)
    pltpu.make_async_remote_copy(
        src_ref=table.at[pl.ds(0, NG - 1)], dst_ref=table_in.at[pl.ds(0, NG - 1)],
        send_sem=table_send, recv_sem=table_recv, device_id=(g, m), device_id_type=MESH,
    ).wait()
    next_word = multiply(BATCHES[0], 0)
    both(far_first)
    both(lambda half: across(half, 0))
    next_word = multiply(BATCHES[1], next_word)
    both(lambda half: across(half, 1))
    both(lambda half: across(half, 3))
    next_word = multiply(BATCHES[2], next_word)
    both(lambda half: across(half, 2))
    both(lambda half: opposite(half, (0,)))
    next_word = multiply(BATCHES[3], next_word)
    both(lambda half: opposite(half, (1, 3, 2)))
    multiply(BATCHES[4], next_word)

    pltpu.make_async_remote_copy(
        src_ref=blocks.at[pl.ds(0, 30)], dst_ref=blocks.at[pl.ds(0, 30)],
        send_sem=gather_send, recv_sem=gather_recv.at[0], device_id=(g, m), device_id_type=MESH,
    ).wait_send()
    pltpu.make_async_copy(words.at[0], words_in.at[0], own_sem).wait()
    pltpu.make_async_remote_copy(
        src_ref=words.at[pl.ds(0, NG - 1)], dst_ref=words_in.at[pl.ds(0, NG - 1)],
        send_sem=word_send, recv_sem=word_recv, device_id=(g, m), device_id_type=MESH,
    ).wait()

    received = words_in[...].reshape(20 * NG, LANES)
    high = received >> 16
    low = (received << 16) >> 16
    scale = jnp.exp2(high[:, 96:97].astype(jnp.float32))
    values = jnp.concatenate([low, high], axis=1).astype(jnp.float32) * scale
    coarse = values.astype(jnp.bfloat16)
    fine = (values - coarse.astype(jnp.float32)).astype(jnp.bfloat16)
    taken = jnp.dot(chooser[...], coarse, preferred_element_type=jnp.float32)
    taken = taken + jnp.dot(chooser[...], fine, preferred_element_type=jnp.float32)
    out_ref[:, 0:224] = taken[0:64, 0:224].astype(jnp.bfloat16)
    out_ref[:, 224:448] = taken[64:128, 0:224].astype(jnp.bfloat16)


def per_device(route_group, expert_pick, route_score, expert_hidden, down_weight):
    any_spec = pl.BlockSpec(memory_space=pl.ANY)
    return pl.pallas_call(
        kernel,
        out_shape=jax.ShapeDtypeStruct((64, 448), jnp.bfloat16),
        in_specs=[any_spec] * 5,
        out_specs=pl.BlockSpec(memory_space=pltpu.VMEM),
        scratch_shapes=[
            pltpu.VMEM((4, 64), jnp.int32),
            pltpu.VMEM((4, 2, 64), jnp.int32),
            pltpu.VMEM((4, 2, 64), jnp.float32),
            pltpu.VMEM((20, 4096), jnp.bfloat16),
            pltpu.VMEM((2, 512, 2048), jnp.bfloat16),
            pltpu.VMEM((2 * NM, ROWS, WIDE), jnp.bfloat16),
            pltpu.VMEM((NG, 1, 2 * LANES), jnp.float32),
            pltpu.VMEM((NG, 1, 2 * LANES), jnp.float32),
            pltpu.VMEM((NG, 5, 4, LANES), jnp.int32),
            pltpu.VMEM((NG, 5, 4, LANES), jnp.int32),
            pltpu.VMEM((LANES, 20 * NG), jnp.bfloat16),
            pltpu.SemaphoreType.DMA((6,)),
            pltpu.SemaphoreType.DMA,
            pltpu.SemaphoreType.DMA((64,)),
            pltpu.SemaphoreType.DMA,
            pltpu.SemaphoreType.DMA,
            pltpu.SemaphoreType.DMA,
            pltpu.SemaphoreType.DMA,
            pltpu.SemaphoreType.DMA,
        ],
        compiler_params=pltpu.CompilerParams(
            collective_id=0, has_side_effects=True, vmem_limit_bytes=40 << 20
        ),
        name="experts_return",
    )(
        jnp.transpose(route_group, (1, 0)),
        jnp.transpose(expert_pick, (1, 2, 0)),
        jnp.transpose(route_score, (1, 2, 0)),
        expert_hidden[0],
        jnp.swapaxes(down_weight[0], 1, 2),
    )


def solution(mesh):
    placed = (
        P("group", None),
        P("group", None, None),
        P("group", None, None),
        P("group", "member", None),
        P("group", None, None, "member"),
    )
    return jax.shard_map(
        per_device, mesh=mesh, in_specs=placed, out_specs=P("group", "member"), check_vma=False
    )
```

time: 202 us -> 54.9 us (0.27)
  the two profiles are of different devices: /device:TPU:1 before, /device:TPU:13 now
where the time goes in v1:
time: 54.9 us; the launch traced here: 54.7 us
  Pallas kernels  49 us (89%)
  local copies, waits for them, and re-layouts  5.65 us (10%)
    pallas_call x1, Pallas kernels, per_device(): pl.pallas_call(kernel, out_shape=jax.ShapeDtypeStruct((64, 448), jnp.bflo...  49 us
    unnamed x11, local copies, waits for them, and re-layouts  5.65 us

profile of v1, /device:TPU:13, one launch (start us, length us, event | category | flops | bytes accessed | tf_op | source)
XLA Modules:
  0.0 54.7 jit_solution(11420102235894728160)
XLA Ops:
  0.0 0.0 copy-start
  0.0 2.0 %copy-done = bf16[1,2,2048,448]{2,3,1,0:T(8,128)(2,1)S(1)} copy-done((bf16[1,2,2048,448]{2,3,1,0:T(8,128)(2,1)S(1)}, bf16[1,2,2048,448]{2,3,1,0:T(8,128)(2,1)}, u32[]{:S(2)}) %copy-start) | copy-done | bytes 3670040
  2.0 0.0 copy-start.1
  2.0 0.9 %copy-done.1 = bf16[1,20,4096]{2,1,0:T(8,128)(2,1)S(1)} copy-done((bf16[1,20,4096]{2,1,0:T(8,128)(2,1)S(1)}, bf16[1,20,4096]{2,1,0:T(8,128)(2,1)}, u32[]{:S(2)}) %copy-start.1) | copy-done | bytes 163864
  3.0 0.0 copy-start.2
  3.0 0.7 %copy-done.2 = s32[64,4,2]{0,2,1:T(2,128)S(1)} copy-done((s32[64,4,2]{0,2,1:T(2,128)S(1)}, s32[64,4,2]{0,2,1:T(2,128)}, u32[]{:S(2)}) %copy-start.2) | copy-done | bytes 2072
  3.7 0.0 copy-start.3
  3.7 0.7 %copy-done.3 = f32[64,4,2]{0,2,1:T(2,128)S(1)} copy-done((f32[64,4,2]{0,2,1:T(2,128)S(1)}, f32[64,4,2]{0,2,1:T(2,128)}, u32[]{:S(2)}) %copy-start.3) | copy-done | bytes 2072
  4.3 0.0 copy-start.4
  4.3 0.7 %copy-done.4 = s32[64,4]{0,1:T(4,128)S(1)} copy-done((s32[64,4]{0,1:T(4,128)S(1)}, s32[64,4]{0,1:T(4,128)}, u32[]{:S(2)}) %copy-start.4) | copy-done | bytes 1048
  5.0 49.0 %experts_return.1 = bf16[64,448]{1,0:T(8,128)(2,1)S(1)} custom-call(s32[4,64]{1,0:T(4,128)S(1)} %bitcast.11, s32[4,2,64]{2,1,0:T(2,128)S(1)} %bitcast.9, f32[4,2,64]{2,1,0:T(2,128)S(1)} %bitcast.10, bf16[20,4096]{1,0:T(8,128)(2,1)S(1)} %bitcast.8, bf16[2,448,2048]{2,1,0:T(8,128)(2,1)S(1)} %bitcast.7), custom_call_target="tpu_custom_call" | custom-call | tf_op jit(solution)/shard_map/experts_return/pallas_call | solution.py:330
  54.0 0.6 %copy.7 = bf16[64,448]{1,0:T(8,128)(2,1)} copy(bf16[64,448]{1,0:T(8,128)(2,1)S(1)} %experts_return.1) | data formatting | bytes 114688
Async XLA Ops:
  0.0 2.0 %copy-start = (bf16[1,2,2048,448]{2,3,1,0:T(8,128)(2,1)S(1)}, bf16[1,2,2048,448]{2,3,1,0:T(8,128)(2,1)}, u32[]{:S(2)}) copy-start(bf16[1,2,2048,448]{2,3,1,0:T(8,128)(2,1)} %param.9) | copy-start | bytes 11010052
  2.0 0.9 %copy-start.1 = (bf16[1,20,4096]{2,1,0:T(8,128)(2,1)S(1)}, bf16[1,20,4096]{2,1,0:T(8,128)(2,1)}, u32[]{:S(2)}) copy-start(bf16[1,20,4096]{2,1,0:T(8,128)(2,1)} %param.8) | copy-start | bytes 491524
  3.0 0.7 %copy-start.2 = (s32[64,4,2]{0,2,1:T(2,128)S(1)}, s32[64,4,2]{0,2,1:T(2,128)}, u32[]{:S(2)}) copy-start(s32[64,4,2]{0,2,1:T(2,128)} %param.6) | copy-start | bytes 6148
  3.7 0.7 %copy-start.3 = (f32[64,4,2]{0,2,1:T(2,128)S(1)}, f32[64,4,2]{0,2,1:T(2,128)}, u32[]{:S(2)}) copy-start(f32[64,4,2]{0,2,1:T(2,128)} %param.7) | copy-start | bytes 6148
  4.3 0.7 %copy-start.4 = (s32[64,4]{0,1:T(4,128)S(1)}, s32[64,4]{0,1:T(4,128)}, u32[]{:S(2)}) copy-start(s32[64,4]{0,1:T(4,128)} %param.5) | copy-start | bytes 3076

commit v2 on v1

--- a/solution.py
+++ b/solution.py
@@ -21,9 +21,9 @@
     ((2, 0), (0, 1), (0, 3)),
     ((1, 1), (3, 1), (1, 3), (3, 3)),
     ((2, 1), (2, 3), (0, 2)),
-    ((1, 2), (3, 2), (2, 2)),
+    ((3, 2), (1, 2)),
+    ((2, 2),),
 )
-ORDER = tuple((half, block) for batch in BATCHES for half in (0, 1) for block in batch)
 
 
 def slot_in_batch(half, first, second):
@@ -37,7 +37,7 @@
 
 def kernel(
     route_hbm, pick_hbm, score_hbm, hidden_hbm, weight_hbm, out_ref,
-    route, pick, score, hidden, weight, blocks, table, table_in, words, words_in, chooser,
+    route, pick, score, hidden, weight, blocks, table, table_in, products, words, words_in, chooser,
     load_sem, gather_send, gather_recv, table_send, table_recv, word_send, word_recv, own_sem,
 ):
     g = lax.axis_index("group")
@@ -68,11 +68,9 @@
     for dx, dy in ((1, 0), (3, 0), (0, 1), (0, 3)):
         pl.semaphore_signal(barrier, inc=1, device_id=(g, member_at(dx, dy)), device_id_type=MESH)
 
-    def greet(i, carry):
-        pl.semaphore_signal(barrier, inc=1, device_id=((g + i) % NG, m), device_id_type=MESH)
-        return carry
-
-    lax.fori_loop(1, NG, greet, 0)
+    far_first = [sign * steps for steps in range(NG // 2, 0, -1) for sign in (1, -1)][1:]
+    for steps in far_first:
+        pl.semaphore_signal(barrier, inc=1, device_id=((g + steps) % NG, m), device_id_type=MESH)
 
     loads[0].wait()
     for half in (0, 1):
@@ -82,54 +80,6 @@
         blocks[mine, :, 4096:WIDE] = jnp.concatenate(
             [hidden[at + 8 : at + 10, q * 1024 : (q + 1) * 1024] for q in range(4)], axis=0
         )
-
-    pl.semaphore_wait(barrier, 4 + NG - 1)
-
-    def offsets(half, du, dv):
-        return (du, dv) if half == 0 else (dv, du)
-
-    def slot_of(half, du, dv):
-        dx, dy = offsets(half, du, dv)
-        return half * NM + member_at(dx, dy)
-
-    def part_of(slot, part):
-        if part is None:
-            return blocks.at[slot]
-        return blocks.at[slot, :, pl.ds(part * HALF, HALF)]
-
-    def copy(half, du, dv, part, su, sv):
-        slot = slot_of(half, du, dv)
-        ref = part_of(slot, part)
-        index = ((half * 4 + (du - su) % 4) * 4 + (dv - sv) % 4) * 2 + (part or 0)
-        return pltpu.make_async_remote_copy(
-            src_ref=ref,
-            dst_ref=ref,
-            send_sem=gather_send,
-            recv_sem=gather_recv.at[index],
-            device_id=(g, member_at(*offsets(half, su, sv))),
-            device_id_type=MESH,
-        )
-
-    def send(half, du, dv, part, su, sv):
-        copy(half, du, dv, part, su, sv).start()
-
-    def arrived(half, du, dv):
-        parts = (0, 1) if 2 in (du, dv) and (dv == 2 or dv == 0) else (None,)
-        for part in parts:
-            slot = slot_of(half, du, dv)
-            ref = part_of(slot, part)
-            index = ((half * 4 + du) * 4 + dv) * 2 + (part or 0)
-            pltpu.make_async_remote_copy(
-                src_ref=ref, dst_ref=ref, send_sem=gather_send, recv_sem=gather_recv.at[index],
-                device_id=(g, m), device_id_type=MESH,
-            ).wait_recv()
-
-    for half in (0, 1):
-        send(half, 0, 0, None, 1, 0)
-        send(half, 0, 0, None, 3, 0)
-    for half in (0, 1):
-        send(half, 0, 0, None, 0, 1)
-        send(half, 0, 0, None, 0, 3)
 
     for load in loads[1:4]:
         load.wait()
@@ -166,16 +116,63 @@
         total = total + jnp.concatenate(both, axis=1)
     table[...] = total.reshape(NG, 1, 2 * LANES)
 
-    def send_table(i, carry):
-        to = (g + i) % NG
+    pl.semaphore_wait(barrier, 4 + NG - 1)
+
+    def offsets(half, du, dv):
+        return (du, dv) if half == 0 else (dv, du)
+
+    def slot_of(half, du, dv):
+        dx, dy = offsets(half, du, dv)
+        return half * NM + member_at(dx, dy)
+
+    def part_of(slot, part):
+        return blocks.at[slot, :, pl.ds(part * HALF, HALF)]
+
+    def copy(half, du, dv, part, su, sv):
+        slot = slot_of(half, du, dv)
+        ref = part_of(slot, part)
+        index = ((half * 4 + (du - su) % 4) * 4 + (dv - sv) % 4) * 2 + part
+        return pltpu.make_async_remote_copy(
+            src_ref=ref,
+            dst_ref=ref,
+            send_sem=gather_send,
+            recv_sem=gather_recv.at[index],
+            device_id=(g, member_at(*offsets(half, su, sv))),
+            device_id_type=MESH,
+        )
+
+    def send(half, du, dv, part, su, sv):
+        copy(half, du, dv, part, su, sv).start()
+
+    def arrived(half, du, dv, part):
+        ref = part_of(slot_of(half, du, dv), part)
+        index = ((half * 4 + du) * 4 + dv) * 2 + part
+        pltpu.make_async_remote_copy(
+            src_ref=ref, dst_ref=ref, send_sem=gather_send, recv_sem=gather_recv.at[index],
+            device_id=(g, m), device_id_type=MESH,
+        ).wait_recv()
+
+    along = ((1, 0), (3, 0))
+    cross = ((0, 1), (0, 3))
+
+    def spread(half, du, dv, parts, targets):
+        for part, (su, sv) in zip(parts, targets):
+            send(half, du, dv, part, su, sv)
+
+    for parts in ((0, 1), (1, 0)):
+        for half in (0, 1):
+            spread(half, 0, 0, parts, along)
+    for steps in far_first:
+        to = (g + steps) % NG
         pltpu.make_async_remote_copy(
             src_ref=table.at[to], dst_ref=table_in.at[g], send_sem=table_send, recv_sem=table_recv,
             device_id=(to, m), device_id_type=MESH,
         ).start()
-        return carry
-
-    lax.fori_loop(1, NG, send_table, 0)
     table_in[g] = table[g]
+
+    for parts in ((0, 1), (1, 0)):
+        for half in (0, 1):
+            spread(half, 0, 0, parts, cross)
 
     row = lax.broadcasted_iota(jnp.int32, (1, 20 * NG), 1)
     piece, inside = (row % 20) // 4, row % 4
@@ -194,34 +191,46 @@
     weight[:, 224:256, :] = jnp.zeros((2, 32, 2048), jnp.bfloat16)
     weight[:, 480:512, :] = jnp.zeros((2, 32, 2048), jnp.bfloat16)
 
-    def multiply(batch, first_word):
-        todo = [(half, du, dv) for half in (0, 1) for du, dv in batch]
+    def blocks_of(batch):
+        return [(half, du, dv) for half in (0, 1) for du, dv in batch]
+
+    def multiply(number):
+        slots = [slot_of(*block) for block in blocks_of(BATCHES[number])]
+        rows = 8 * len(slots)
+        rest = [blocks[s, :, 4096:WIDE] for s in slots]
+        line = lax.broadcasted_iota(jnp.int32, (2 * rows, 1), 0)
+        for e in range(2):
+            result = None
+            for q in (2 * e, 2 * e + 1):
+                left = jnp.concatenate(
+                    [blocks[s, :, q * 1024 : (q + 1) * 1024] for s in slots] + rest, axis=0
+                )
+                product = lax.dot_general(
+                    left, weight[e, :, (q % 2) * 1024 : (q % 2 + 1) * 1024],
+                    (((1,), (1,)), ((), ())), preferred_element_type=jnp.float32,
+                )
+                product = jnp.where((line < rows) | ((line % 8) // 2 == q), product, 0.0)
+                result = product if result is None else result + product
+            products[number, e, 0:rows] = result[:rows]
+            products[number, e, MAIN : MAIN + rows] = result[rows:]
+
+    def finish(number):
+        todo = blocks_of(BATCHES[number])
         count = len(todo)
-        slots = [slot_of(*block) for block in todo]
-        padded = slots + [slots[0]] * (8 - count)
+        first_word = sum(2 * len(batch) for batch in BATCHES[:number])
         coefs = None
         for half, du, dv in todo:
             home = 2 * member_at(*offsets(half, du, dv)) + half
             coefs = table_in[home] if coefs is None else coefs + table_in[home]
-        each = []
-        for q in range(4):
-            part = coefs[:, (q // 2) * LANES : (q // 2 + 1) * LANES]
-            each.append(jnp.where((lane < MAIN) | (inner // 2 == q), part, 0.0))
-        columns = jnp.transpose(jnp.concatenate(each + each, axis=0), (1, 0))
-        rest = [blocks[s, :, 4096:WIDE] for s in padded]
-        result = None
-        for q in range(4):
-            left = jnp.concatenate(
-                [blocks[s, :, q * 1024 : (q + 1) * 1024] for s in padded] + rest, axis=0
-            )
-            product = lax.dot_general(
-                left, weight[q // 2, :, (q % 2) * 1024 : (q % 2 + 1) * 1024],
-                (((1,), (1,)), ((), ())), preferred_element_type=jnp.float32,
-            )
-            product = product * columns[:, q : q + 1]
-            result = product if result is None else result + product
-        main = result[0 : 8 * count]
-        tail = result[MAIN : MAIN + 8 * count]
+        rows = [coefs[:, :LANES], coefs[:, LANES:]] * 4
+        columns = jnp.transpose(jnp.concatenate(rows, axis=0), (1, 0))
+
+        def weighted(at):
+            rows = slice(at, at + 8 * count)
+            first = products[number, 0, rows] * columns[rows, 0:1]
+            return first + products[number, 1, rows] * columns[rows, 1:2]
+
+        main, tail = weighted(0), weighted(MAIN)
         tail = tail + pltpu.roll(tail, 8 * count - 4, 0)
         tail = tail + pltpu.roll(tail, 8 * count - 2, 0)
         for rows, is_tail in ((main, False), (tail, True)):
@@ -254,53 +263,85 @@
             def _():
                 pltpu.make_async_copy(words.at[first_word + j], words_in.at[g], own_sem).start()
 
-        return first_word + count
-
-    def both(step):
-        for half in (0, 1):
-            step(half)
-
-    def near_first(half):
-        arrived(half, 1, 0)
-        arrived(half, 3, 0)
+    def pass_along(half):
+        arrived(half, 3, 0, 0)
+        arrived(half, 1, 0, 1)
         send(half, 3, 0, 0, 1, 0)
         send(half, 1, 0, 1, 3, 0)
-        for du in (1, 3):
-            for sv in (1, 3):
-                send(half, du, 0, None, 0, sv)
-
-    def across(half, du):
-        arrived(half, du, 1)
-        arrived(half, du, 3)
+
+    def pass_cross(half, du):
+        arrived(half, du, 3, 0)
+        arrived(half, du, 1, 1)
         send(half, du, 3, 0, 0, 1)
         send(half, du, 1, 1, 0, 3)
 
-    def far_first(half):
-        arrived(half, 2, 0)
-        for sv in (1, 3):
-            send(half, 2, 0, None, 0, sv)
-
-    def opposite(half, dus):
-        for du in dus:
-            arrived(half, du, 2)
-
-    both(near_first)
-    pltpu.make_async_remote_copy(
+    def rest_cross(half, du):
+        arrived(half, du, 3, 1)
+        arrived(half, du, 1, 0)
+
+    def opposite(half, du):
+        arrived(half, du, 2, 0)
+        arrived(half, du, 2, 1)
+
+    halves = (0, 1)
+    for half in halves:
+        pass_along(half)
+    for half in halves:
+        spread(half, 3, 0, (0, 0), cross)
+        spread(half, 1, 0, (1, 1), cross[::-1])
+    for half in halves:
+        arrived(half, 3, 0, 1)
+        arrived(half, 1, 0, 0)
+        spread(half, 3, 0, (1, 1), cross[::-1])
+        spread(half, 1, 0, (0, 0), cross)
+    multiply(0)
+    for half in halves:
+        pass_cross(half, 0)
+    for half in halves:
+        arrived(half, 2, 0, 0)
+        arrived(half, 2, 0, 1)
+        spread(half, 2, 0, (0, 1), cross)
+        spread(half, 2, 0, (1, 0), cross)
+    for du in (0,):
+        for half in halves:
+            rest_cross(half, du)
+    multiply(1)
+    for du in (3, 1):
+        for half in halves:
+            pass_cross(half, du)
+    tables = pltpu.make_async_remote_copy(
         src_ref=table.at[pl.ds(0, NG - 1)], dst_ref=table_in.at[pl.ds(0, NG - 1)],
         send_sem=table_send, recv_sem=table_recv, device_id=(g, m), device_id_type=MESH,
-    ).wait()
-    next_word = multiply(BATCHES[0], 0)
-    both(far_first)
-    both(lambda half: across(half, 0))
-    next_word = multiply(BATCHES[1], next_word)
-    both(lambda half: across(half, 1))
-    both(lambda half: across(half, 3))
-    next_word = multiply(BATCHES[2], next_word)
-    both(lambda half: across(half, 2))
-    both(lambda half: opposite(half, (0,)))
-    next_word = multiply(BATCHES[3], next_word)
-    both(lambda half: opposite(half, (1, 3, 2)))
-    multiply(BATCHES[4], next_word)
+    )
+    tables.wait_recv()
+    finish(0)
+    finish(1)
+    for du in (3, 1):
+        for half in halves:
+            rest_cross(half, du)
+    multiply(2)
+    finish(2)
+    for half in halves:
+        pass_cross(half, 2)
+    for du in (2,):
+        for half in halves:
+            rest_cross(half, du)
+    for du in (0,):
+        for half in halves:
+            opposite(half, du)
+    multiply(3)
+    finish(3)
+    for du in (3, 1):
+        for half in halves:
+            opposite(half, du)
+    multiply(4)
+    finish(4)
+    for du in (2,):
+        for half in halves:
+            opposite(half, du)
+    multiply(5)
+    finish(5)
+    tables.wait_send()
 
     pltpu.make_async_remote_copy(
         src_ref=blocks.at[pl.ds(0, 30)], dst_ref=blocks.at[pl.ds(0, 30)],
@@ -326,11 +367,11 @@
 
 
 def per_device(route_group, expert_pick, route_score, expert_hidden, down_weight):
-    any_spec = pl.BlockSpec(memory_space=pl.ANY)
+    hbm = pl.BlockSpec(memory_space=pl.ANY)
     return pl.pallas_call(
         kernel,
         out_shape=jax.ShapeDtypeStruct((64, 448), jnp.bfloat16),
-        in_specs=[any_spec] * 5,
+        in_specs=[hbm] * 5,
         out_specs=pl.BlockSpec(memory_space=pltpu.VMEM),
         scratch_shapes=[
             pltpu.VMEM((4, 64), jnp.int32),
@@ -341,6 +382,7 @@
             pltpu.VMEM((2 * NM, ROWS, WIDE), jnp.bfloat16),
             pltpu.VMEM((NG, 1, 2 * LANES), jnp.float32),
             pltpu.VMEM((NG, 1, 2 * LANES), jnp.float32),
+            pltpu.VMEM((len(BATCHES), 2, LANES, 512), jnp.float32),
             pltpu.VMEM((NG, 5, 4, LANES), jnp.int32),
             pltpu.VMEM((NG, 5, 4, LANES), jnp.int32),
             pltpu.VMEM((LANES, 20 * NG), jnp.bfloat16),
@@ -354,7 +396,7 @@
             pltpu.SemaphoreType.DMA,
         ],
         compiler_params=pltpu.CompilerParams(
-            collective_id=0, has_side_effects=True, vmem_limit_bytes=40 << 20
+            collective_id=0, has_side_effects=True, vmem_limit_bytes=63 << 20
         ),
         name="experts_return",
     )(

time: 54.9 us -> 48.5 us (0.88)
  the two profiles are of different devices: /device:TPU:13 before, /device:TPU:21 now
where the time goes in v2:
time: 48.5 us; the launch traced here: 48.3 us
  Pallas kernels  46.8 us (96%)
  local copies, waits for them, and re-layouts  1.47 us (3%)
    pallas_call x1, Pallas kernels, per_device(): pl.pallas_call(kernel, out_shape=jax.ShapeDtypeStruct((64, 448), jnp.bflo...  46.8 us
    unnamed x1, local copies, waits for them, and re-layouts  1.47 us

profile of v2, /device:TPU:21, one launch (start us, length us, event | category | flops | bytes accessed | tf_op | source)
XLA Modules:
  0.0 48.3 jit_solution(4416049208654828749)
XLA Ops:
  0.0 46.8 %experts_return.1 = bf16[64,448]{1,0:T(8,128)(2,1)} custom-call(s32[4,64]{1,0:T(4,128)} %bitcast.11, s32[4,2,64]{2,1,0:T(2,128)} %bitcast.9, f32[4,2,64]{2,1,0:T(2,128)} %bitcast.10, bf16[20,4096]{1,0:T(8,128)(2,1)} %bitcast.8, bf16[2,448,2048]{2,1,0:T(8,128)(2,1)} %bitcast.7), custom_call_target="tpu_custom_call" | custom-call | tf_op jit(solution)/shard_map/experts_return/pallas_call | solution.py:371
  46.9 1.5 %copy.7 = bf16[64,448]{1,0:T(8,128)(2,1)} copy(bf16[64,448]{1,0:T(8,128)(2,1)} %experts_return.1) | data formatting | bytes 114688

commit v3 on v2

--- a/solution.py
+++ b/solution.py
@@ -39,6 +39,7 @@
     route_hbm, pick_hbm, score_hbm, hidden_hbm, weight_hbm, out_ref,
     route, pick, score, hidden, weight, blocks, table, table_in, products, words, words_in, chooser,
     load_sem, gather_send, gather_recv, table_send, table_recv, word_send, word_recv, own_sem,
+    round_sem,
 ):
     g = lax.axis_index("group")
     m = lax.axis_index("member")
@@ -68,9 +69,12 @@
     for dx, dy in ((1, 0), (3, 0), (0, 1), (0, 3)):
         pl.semaphore_signal(barrier, inc=1, device_id=(g, member_at(dx, dy)), device_id_type=MESH)
 
-    far_first = [sign * steps for steps in range(NG // 2, 0, -1) for sign in (1, -1)][1:]
-    for steps in far_first:
-        pl.semaphore_signal(barrier, inc=1, device_id=((g + steps) % NG, m), device_id_type=MESH)
+    def along_z(steps):
+        return (g + 2 * steps) % NG
+
+    other_core = g + 1 - 2 * core
+    for to in [along_z(steps) for steps in (2, -2, 1, -1)] + [other_core]:
+        pl.semaphore_signal(barrier, inc=1, device_id=(to, m), device_id_type=MESH)
 
     loads[0].wait()
     for half in (0, 1):
@@ -80,6 +84,65 @@
         blocks[mine, :, 4096:WIDE] = jnp.concatenate(
             [hidden[at + 8 : at + 10, q * 1024 : (q + 1) * 1024] for q in range(4)], axis=0
         )
+
+    pl.semaphore_wait(barrier, 9)
+
+    def tell(step, targets):
+        for to in targets:
+            pl.semaphore_signal(round_sem.at[step], inc=1, device_id=(to, m), device_id_type=MESH)
+
+    def told(step, count):
+        pl.semaphore_wait(round_sem.at[step], count)
+
+    tell(0, [along_z(steps) for steps in (2, -2, 1, -1)])
+
+    def offsets(half, du, dv):
+        return (du, dv) if half == 0 else (dv, du)
+
+    def slot_of(half, du, dv):
+        dx, dy = offsets(half, du, dv)
+        return half * NM + member_at(dx, dy)
+
+    def part_of(slot, part):
+        return blocks.at[slot, :, pl.ds(part * HALF, HALF)]
+
+    def copy(half, du, dv, part, su, sv):
+        slot = slot_of(half, du, dv)
+        ref = part_of(slot, part)
+        index = ((half * 4 + (du - su) % 4) * 4 + (dv - sv) % 4) * 2 + part
+        return pltpu.make_async_remote_copy(
+            src_ref=ref,
+            dst_ref=ref,
+            send_sem=gather_send,
+            recv_sem=gather_recv.at[index],
+            device_id=(g, member_at(*offsets(half, su, sv))),
+            device_id_type=MESH,
+        )
+
+    def send(half, du, dv, part, su, sv):
+        copy(half, du, dv, part, su, sv).start()
+
+    def arrived(half, du, dv, part):
+        ref = part_of(slot_of(half, du, dv), part)
+        index = ((half * 4 + du) * 4 + dv) * 2 + part
+        pltpu.make_async_remote_copy(
+            src_ref=ref, dst_ref=ref, send_sem=gather_send, recv_sem=gather_recv.at[index],
+            device_id=(g, m), device_id_type=MESH,
+        ).wait_recv()
+
+    along = ((1, 0), (3, 0))
+    cross = ((0, 1), (0, 3))
+
+    def spread(half, du, dv, parts, targets):
+        for part, (su, sv) in zip(parts, targets):
+            send(half, du, dv, part, su, sv)
+
+    for parts in ((0, 1), (1, 0)):
+        for half in (0, 1):
+            spread(half, 0, 0, parts, along)
+    for parts in ((0, 1), (1, 0)):
+        for half in (0, 1):
+            spread(half, 0, 0, parts, cross)
 
     for load in loads[1:4]:
         load.wait()
@@ -116,63 +179,8 @@
         total = total + jnp.concatenate(both, axis=1)
     table[...] = total.reshape(NG, 1, 2 * LANES)
 
-    pl.semaphore_wait(barrier, 4 + NG - 1)
-
-    def offsets(half, du, dv):
-        return (du, dv) if half == 0 else (dv, du)
-
-    def slot_of(half, du, dv):
-        dx, dy = offsets(half, du, dv)
-        return half * NM + member_at(dx, dy)
-
-    def part_of(slot, part):
-        return blocks.at[slot, :, pl.ds(part * HALF, HALF)]
-
-    def copy(half, du, dv, part, su, sv):
-        slot = slot_of(half, du, dv)
-        ref = part_of(slot, part)
-        index = ((half * 4 + (du - su) % 4) * 4 + (dv - sv) % 4) * 2 + part
-        return pltpu.make_async_remote_copy(
-            src_ref=ref,
-            dst_ref=ref,
-            send_sem=gather_send,
-            recv_sem=gather_recv.at[index],
-            device_id=(g, member_at(*offsets(half, su, sv))),
-            device_id_type=MESH,
-        )
-
-    def send(half, du, dv, part, su, sv):
-        copy(half, du, dv, part, su, sv).start()
-
-    def arrived(half, du, dv, part):
-        ref = part_of(slot_of(half, du, dv), part)
-        index = ((half * 4 + du) * 4 + dv) * 2 + part
-        pltpu.make_async_remote_copy(
-            src_ref=ref, dst_ref=ref, send_sem=gather_send, recv_sem=gather_recv.at[index],
-            device_id=(g, m), device_id_type=MESH,
-        ).wait_recv()
-
-    along = ((1, 0), (3, 0))
-    cross = ((0, 1), (0, 3))
-
-    def spread(half, du, dv, parts, targets):
-        for part, (su, sv) in zip(parts, targets):
-            send(half, du, dv, part, su, sv)
-
-    for parts in ((0, 1), (1, 0)):
-        for half in (0, 1):
-            spread(half, 0, 0, parts, along)
-    for steps in far_first:
-        to = (g + steps) % NG
-        pltpu.make_async_remote_copy(
-            src_ref=table.at[to], dst_ref=table_in.at[g], send_sem=table_send, recv_sem=table_recv,
-            device_id=(to, m), device_id_type=MESH,
-        ).start()
-    table_in[g] = table[g]
-
-    for parts in ((0, 1), (1, 0)):
-        for half in (0, 1):
-            spread(half, 0, 0, parts, cross)
+    told(0, 4)
+    tell(1, [along_z(steps) for steps in (4, -4, 3, -3)])
 
     row = lax.broadcasted_iota(jnp.int32, (1, 20 * NG), 1)
     piece, inside = (row % 20) // 4, row % 4
@@ -294,9 +302,19 @@
         arrived(half, 1, 0, 0)
         spread(half, 3, 0, (1, 1), cross[::-1])
         spread(half, 1, 0, (0, 0), cross)
+    told(1, 4)
+    tell(2, [other_core])
+    told(2, 1)
+    for steps in [sign * steps for steps in range(NG // 2, 0, -1) for sign in (1, -1)][1:]:
+        to = (g + steps) % NG
+        pltpu.make_async_remote_copy(
+            src_ref=table.at[to], dst_ref=table_in.at[g], send_sem=table_send, recv_sem=table_recv,
+            device_id=(to, m), device_id_type=MESH,
+        ).start()
+    table_in[g] = table[g]
+    for half in halves:
+        pass_cross(half, 0)
     multiply(0)
-    for half in halves:
-        pass_cross(half, 0)
     for half in halves:
         arrived(half, 2, 0, 0)
         arrived(half, 2, 0, 1)
@@ -309,6 +327,12 @@
     for du in (3, 1):
         for half in halves:
             pass_cross(half, du)
+    for du in (3, 1):
+        for half in halves:
+            rest_cross(half, du)
+    multiply(2)
+    for half in halves:
+        pass_cross(half, 2)
     tables = pltpu.make_async_remote_copy(
         src_ref=table.at[pl.ds(0, NG - 1)], dst_ref=table_in.at[pl.ds(0, NG - 1)],
         send_sem=table_send, recv_sem=table_recv, device_id=(g, m), device_id_type=MESH,
@@ -316,13 +340,7 @@
     tables.wait_recv()
     finish(0)
     finish(1)
-    for du in (3, 1):
-        for half in halves:
-            rest_cross(half, du)
-    multiply(2)
     finish(2)
-    for half in halves:
-        pass_cross(half, 2)
     for du in (2,):
         for half in halves:
             rest_cross(half, du)
@@ -394,6 +412,7 @@
             pltpu.SemaphoreType.DMA,
             pltpu.SemaphoreType.DMA,
             pltpu.SemaphoreType.DMA,
+            pltpu.SemaphoreType.REGULAR((3,)),
         ],
         compiler_params=pltpu.CompilerParams(
             collective_id=0, has_side_effects=True, vmem_limit_bytes=63 << 20

time: 48.5 us -> 46.8 us (0.965)
  the two profiles are of different devices: /device:TPU:21 before, /device:TPU:39 now
where the time goes in v3:
time: 46.8 us; the launch traced here: 46.7 us
  Pallas kernels  45.2 us (97%)
  local copies, waits for them, and re-layouts  1.47 us (3%)
    pallas_call x1, Pallas kernels, per_device(): pl.pallas_call(kernel, out_shape=jax.ShapeDtypeStruct((64, 448), jnp.bflo...  45.2 us
    unnamed x1, local copies, waits for them, and re-layouts  1.47 us

profile of v3, /device:TPU:39, one launch (start us, length us, event | category | flops | bytes accessed | tf_op | source)
XLA Modules:
  0.0 46.7 jit_solution(5468778922034658867)
XLA Ops:
  0.0 45.2 %experts_return.1 = bf16[64,448]{1,0:T(8,128)(2,1)} custom-call(s32[4,64]{1,0:T(4,128)} %bitcast.11, s32[4,2,64]{2,1,0:T(2,128)} %bitcast.9, f32[4,2,64]{2,1,0:T(2,128)} %bitcast.10, bf16[20,4096]{1,0:T(8,128)(2,1)} %bitcast.8, bf16[2,448,2048]{2,1,0:T(8,128)(2,1)} %bitcast.7), custom_call_target="tpu_custom_call" | custom-call | tf_op jit(solution)/shard_map/experts_return/pallas_call | solution.py:389
  45.2 1.5 %copy.7 = bf16[64,448]{1,0:T(8,128)(2,1)} copy(bf16[64,448]{1,0:T(8,128)(2,1)} %experts_return.1) | data formatting | bytes 114688

commit v4 on v3

--- a/solution.py
+++ b/solution.py
@@ -76,6 +76,17 @@
     for to in [along_z(steps) for steps in (2, -2, 1, -1)] + [other_core]:
         pl.semaphore_signal(barrier, inc=1, device_id=(to, m), device_id_type=MESH)
 
+    pl.semaphore_wait(barrier, 9)
+
+    def tell(step, targets):
+        for to in targets:
+            pl.semaphore_signal(round_sem.at[step], inc=1, device_id=(to, m), device_id_type=MESH)
+
+    def told(step, count):
+        pl.semaphore_wait(round_sem.at[step], count)
+
+    tell(0, [along_z(steps) for steps in (2, -2, 1, -1)])
+
     loads[0].wait()
     for half in (0, 1):
         at = 10 * half
@@ -84,17 +95,6 @@
         blocks[mine, :, 4096:WIDE] = jnp.concatenate(
             [hidden[at + 8 : at + 10, q * 1024 : (q + 1) * 1024] for q in range(4)], axis=0
         )
-
-    pl.semaphore_wait(barrier, 9)
-
-    def tell(step, targets):
-        for to in targets:
-            pl.semaphore_signal(round_sem.at[step], inc=1, device_id=(to, m), device_id_type=MESH)
-
-    def told(step, count):
-        pl.semaphore_wait(round_sem.at[step], count)
-
-    tell(0, [along_z(steps) for steps in (2, -2, 1, -1)])
 
     def offsets(half, du, dv):
         return (du, dv) if half == 0 else (dv, du)
@@ -206,7 +206,7 @@
         slots = [slot_of(*block) for block in blocks_of(BATCHES[number])]
         rows = 8 * len(slots)
         rest = [blocks[s, :, 4096:WIDE] for s in slots]
-        line = lax.broadcasted_iota(jnp.int32, (2 * rows, 1), 0)
+        line = lax.broadcasted_iota(jnp.int32, (rows, 1), 0)
         for e in range(2):
             result = None
             for q in (2 * e, 2 * e + 1):
@@ -217,10 +217,11 @@
                     left, weight[e, :, (q % 2) * 1024 : (q % 2 + 1) * 1024],
                     (((1,), (1,)), ((), ())), preferred_element_type=jnp.float32,
                 )
-                product = jnp.where((line < rows) | ((line % 8) // 2 == q), product, 0.0)
-                result = product if result is None else result + product
-            products[number, e, 0:rows] = result[:rows]
-            products[number, e, MAIN : MAIN + rows] = result[rows:]
+                wanted = jnp.where((line % 8) // 2 == q, product[rows:], 0.0)
+                pair = (product[:rows], wanted)
+                result = pair if result is None else [a + b for a, b in zip(result, pair)]
+            products[number, e, 0:rows] = result[0]
+            products[number, e, MAIN : MAIN + rows] = result[1]
 
     def finish(number):
         todo = blocks_of(BATCHES[number])
@@ -359,12 +360,7 @@
             opposite(half, du)
     multiply(5)
     finish(5)
-    tables.wait_send()
-
-    pltpu.make_async_remote_copy(
-        src_ref=blocks.at[pl.ds(0, 30)], dst_ref=blocks.at[pl.ds(0, 30)],
-        send_sem=gather_send, recv_sem=gather_recv.at[0], device_id=(g, m), device_id_type=MESH,
-    ).wait_send()
+
     pltpu.make_async_copy(words.at[0], words_in.at[0], own_sem).wait()
     pltpu.make_async_remote_copy(
         src_ref=words.at[pl.ds(0, NG - 1)], dst_ref=words_in.at[pl.ds(0, NG - 1)],
@@ -382,6 +378,12 @@
     taken = taken + jnp.dot(chooser[...], fine, preferred_element_type=jnp.float32)
     out_ref[:, 0:224] = taken[0:64, 0:224].astype(jnp.bfloat16)
     out_ref[:, 224:448] = taken[64:128, 0:224].astype(jnp.bfloat16)
+
+    pltpu.make_async_remote_copy(
+        src_ref=blocks.at[pl.ds(0, 30)], dst_ref=blocks.at[pl.ds(0, 30)],
+        send_sem=gather_send, recv_sem=gather_recv.at[0], device_id=(g, m), device_id_type=MESH,
+    ).wait_send()
+    tables.wait_send()
 
 
 def per_device(route_group, expert_pick, route_score, expert_hidden, down_weight):

time: 46.8 us -> 46.8 us (level)
  no operation moved by 1% of the time
where the time goes in v4:
time: 46.8 us; the launch traced here: 46.6 us
  Pallas kernels  45.2 us (97%)
  local copies, waits for them, and re-layouts  1.47 us (3%)
    pallas_call x1, Pallas kernels, per_device(): pl.pallas_call(kernel, out_shape=jax.ShapeDtypeStruct((64, 448), jnp.bflo...  45.2 us
    unnamed x1, local copies, waits for them, and re-layouts  1.47 us

profile of v4, /device:TPU:39, one launch (start us, length us, event | category | flops | bytes accessed | tf_op | source)
XLA Modules:
  0.0 46.6 jit_solution(21577430220015915)
XLA Ops:
  0.0 45.2 %experts_return.1 = bf16[64,448]{1,0:T(8,128)(2,1)} custom-call(s32[4,64]{1,0:T(4,128)} %bitcast.11, s32[4,2,64]{2,1,0:T(2,128)} %bitcast.9, f32[4,2,64]{2,1,0:T(2,128)} %bitcast.10, bf16[20,4096]{1,0:T(8,128)(2,1)} %bitcast.8, bf16[2,448,2048]{2,1,0:T(8,128)(2,1)} %bitcast.7), custom_call_target="tpu_custom_call" | custom-call | tf_op jit(solution)/shard_map/experts_return/pallas_call | solution.py:391
  45.2 1.5 %copy.7 = bf16[64,448]{1,0:T(8,128)(2,1)} copy(bf16[64,448]{1,0:T(8,128)(2,1)} %experts_return.1) | data formatting | bytes 114688
